TPU v7x, 32 devices: a whole 2x2x4 slice. The times are simulated.
32 devices in a mesh: grid: 8 (over z, y), chan: 4 (over x, core).
Axes of the slice: x: 2, y: 2, z: 4, core: 2. Of those that a mesh axis runs over, the one named last changes fastest.
Arguments:
- spectra: bfloat16 [2, 8, 24, 4096], P(None, None, 'grid', 'chan'), may hold values from -90 to 90, as said below
- travel: int32 [32768, 4096], P('grid', 'chan'), may hold values from 0 to 2047
- quality: int32 [4096], P('chan'), may hold values 0 or 1
Outputs:
- beam_power: float32 [24, 32768], P(None, ('grid', 'chan'))
Inputs may be any that keep to these rules, and one draw needn't show every extreme that they name: `spectra`: spectra of the windows; scales differ between channels and between windows.
All inputs are finite; a program needn't handle non-finite values. No bound on the sum of `quality` on one device may be relied on, other than what follows from the above.
Results may differ from a plain program's by a relative error of at most 0.0012.
Values may be sent and summed in bfloat16 or wider, within the bound.
A program may use at most 128 MiB of HBM per device.

v0:
```python
import math

import jax
import jax.numpy as jnp
from jax import lax
from jax.sharding import PartitionSpec as P

NFFT = 2048


lowest_bin = 37
bin_spacing = 29


def replica_rows(delay_rows, freq_count):
    freq_bins = lowest_bin + bin_spacing * jnp.arange(freq_count, dtype=jnp.int32)
    phase_index = freq_bins[:, None, None] * delay_rows[None, :, :] % NFFT
    angles = phase_index.astype(jnp.float32) * (2.0 * math.pi / NFFT)
    return jnp.concatenate([jnp.cos(angles), jnp.sin(angles)], axis=2).astype(jnp.bfloat16)


def stacked_spectra(masked):
    real_part = masked[0]
    imag_part = masked[1]
    upper_half = jnp.concatenate([real_part, imag_part], axis=1)
    lower_half = jnp.concatenate([-imag_part, real_part], axis=1)
    return jnp.concatenate([upper_half, lower_half], axis=2)


def beams_for(delay_table, spectra_matrix, freq_count):
    total_rows = delay_table.shape[0]
    chan_width = delay_table.shape[1]
    block_rows = math.gcd(total_rows, 1024)

    def one_block(delay_rows):
        replicas = replica_rows(delay_rows, freq_count)
        beam_terms = jnp.einsum(
            "frk,fwk->rfw", replicas, spectra_matrix, preferred_element_type=jnp.float32
        )
        return beam_terms.reshape(block_rows, -1)

    block_terms = lax.map(
        one_block, delay_table.reshape(total_rows // block_rows, block_rows, chan_width)
    )
    return block_terms.reshape(total_rows, -1)


def per_device(spectra, travel, quality):
    freq_count = spectra.shape[1]
    masked = spectra * quality.astype(jnp.bfloat16)
    channel_count = masked.shape[3] * lax.axis_size("chan")
    gathered = lax.all_gather(masked, "grid", axis=2, tiled=True)
    window_count = gathered.shape[2]
    norm_sum = lax.psum(jnp.sum(gathered.astype(jnp.float32) ** 2, axis=(0, 1, 3)), "chan")
    window_norm = norm_sum / (freq_count * channel_count) + 1e-06
    rows_out = travel.shape[0] // lax.axis_size("chan")
    spectra_matrix = stacked_spectra(gathered)
    beam_sums = lax.psum_scatter(
        beams_for(travel, spectra_matrix, freq_count), "chan", scatter_dimension=0, tiled=True
    )
    energies = jnp.sum(beam_sums.reshape(rows_out, 2 * freq_count, window_count) ** 2, axis=1)
    beam_power = energies / (freq_count * channel_count * window_norm[None, :])
    return beam_power.T


def solution(mesh):
    return jax.shard_map(
        per_device,
        mesh=mesh,
        in_specs=(P(None, None, "grid", "chan"), P("grid", "chan"), P("chan")),
        out_specs=P(None, ("grid", "chan")),
        check_vma=False,
    )
```

profile of v0, /device:TPU:0, one launch (start us, length us, event | category | flops | bytes accessed | tf_op | source)
XLA Modules:
  0.0 734.8 jit_solution(17397077278311623147)
XLA Ops:
  6.5 0.7 convert_element_type.16
  7.2 0.9 copy_multiply_fusion
  8.1 33.8 %all_gather.3 = bf16[2,8,24,1024]{3,1,0,2:T(8,128)(2,1)S(1)} all-gather(bf16[2,8,3,1024]{3,1,0,2:T(8,128)(2,1)S(1)} %copy_multiply_fusion), channel_id=1, replica_groups=mesh['grid'=8,'chan'=4] {'grid'}, dimensions={2}, use_global_device_ids=true | all-gather | bytes 884736 | tf_op jit(solution)/shard_map/all_gather | solution.py:52
  41.9 0.9 copy-done
  43.0 2.0 copy.10
  45.0 620.0 %while.12 = (s32[]{:T(128)}, f32[4,1024,384]{2,1,0:T(8,128)}, s32[4,1024,1024]{2,1,0:T(8,128)}, bf16[8,48,2048]{2,1,0:T(8,128)(2,1)}, s32[]{:T(128)}) while((s32[]{:T(128)}, f32[4,1024,384]{2,1,0:T(8,128)}, s32[4,1024,1024]{2,1,0:T(8,128)}, bf16[8,48,2048]{2,1,0:T(8,128)(2,1)}, s32[]{:T(128)}) %tuple.36), condition=%wide.region_1.0_spmd, body=%wide.region_0.0_spmd.sunk | while | flops 1811939328 | bytes 89129104 | solution.py:42
  45.0 2.7 dynamic-slice_bitcast_fusion.2
  47.7 135.1 %cosine_convert_fusion.2 = (bf16[8,1024,1024]{2,1,0:T(8,128)(2,1)}, bf16[8,1024,1024]{2,1,0:T(8,128)(2,1)}) fusion(s32[1024,1024]{1,0:T(8,128)S(1)} %dynamic-slice_bitcast_fusion.2, s32[8]{0:T(128)S(1)} %multiply_add_fusion.2), kind=kLoop, calls=%fused_computation.13.clone.1 | loop fusion | flops 134217728 | bytes 37748768 | tf_op jit(solution)/shard_map/convert
  182.8 15.5 %fusion.15 = f32[8,1024,48]{1,2,0:T(8,128)S(1)} fusion(bf16[8,48,2048]{2,1,0:T(8,128)(2,1)} %get-tuple-element.118, bf16[8,1024,1024]{2,1,0:T(8,128)(2,1)} %get-tuple-element.103, bf16[8,1024,1024]{2,1,0:T(8,128)(2,1)} %get-tuple-element.104), kind=kOutput, calls=%fused_computation.8.clone.1 | convolution fusion | flops 1677721600 | bytes 36700160 | tf_op jit(solution)/shard_map/while/body/eval_jaxpr/frk,fwk->rfw/dot_general | solution.py:37
  198.3 0.5 copy.20
  198.8 1.2 constant_dynamic-update-slice_fusion.2
  200.0 2.7 dynamic-slice_bitcast_fusion.2
  202.7 135.1 %cosine_convert_fusion.2 = (bf16[8,1024,1024]{2,1,0:T(8,128)(2,1)}, bf16[8,1024,1024]{2,1,0:T(8,128)(2,1)}) fusion(s32[1024,1024]{1,0:T(8,128)S(1)} %dynamic-slice_bitcast_fusion.2, s32[8]{0:T(128)S(1)} %multiply_add_fusion.2), kind=kLoop, calls=%fused_computation.13.clone.1 | loop fusion | flops 134217728 | bytes 37748768 | tf_op jit(solution)/shard_map/convert
  337.8 15.5 %fusion.15 = f32[8,1024,48]{1,2,0:T(8,128)S(1)} fusion(bf16[8,48,2048]{2,1,0:T(8,128)(2,1)} %get-tuple-element.118, bf16[8,1024,1024]{2,1,0:T(8,128)(2,1)} %get-tuple-element.103, bf16[8,1024,1024]{2,1,0:T(8,128)(2,1)} %get-tuple-element.104), kind=kOutput, calls=%fused_computation.8.clone.1 | convolution fusion | flops 1677721600 | bytes 36700160 | tf_op jit(solution)/shard_map/while/body/eval_jaxpr/frk,fwk->rfw/dot_general | solution.py:37
  353.3 0.5 copy.20
  353.8 1.2 constant_dynamic-update-slice_fusion.2
  355.0 2.7 dynamic-slice_bitcast_fusion.2
  357.7 135.1 %cosine_convert_fusion.2 = (bf16[8,1024,1024]{2,1,0:T(8,128)(2,1)}, bf16[8,1024,1024]{2,1,0:T(8,128)(2,1)}) fusion(s32[1024,1024]{1,0:T(8,128)S(1)} %dynamic-slice_bitcast_fusion.2, s32[8]{0:T(128)S(1)} %multiply_add_fusion.2), kind=kLoop, calls=%fused_computation.13.clone.1 | loop fusion | flops 134217728 | bytes 37748768 | tf_op jit(solution)/shard_map/convert
  492.8 15.5 %fusion.15 = f32[8,1024,48]{1,2,0:T(8,128)S(1)} fusion(bf16[8,48,2048]{2,1,0:T(8,128)(2,1)} %get-tuple-element.118, bf16[8,1024,1024]{2,1,0:T(8,128)(2,1)} %get-tuple-element.103, bf16[8,1024,1024]{2,1,0:T(8,128)(2,1)} %get-tuple-element.104), kind=kOutput, calls=%fused_computation.8.clone.1 | convolution fusion | flops 1677721600 | bytes 36700160 | tf_op jit(solution)/shard_map/while/body/eval_jaxpr/frk,fwk->rfw/dot_general | solution.py:37
  508.3 0.5 copy.20
  508.7 1.3 constant_dynamic-update-slice_fusion.2
  510.1 2.7 dynamic-slice_bitcast_fusion.2
  512.7 135.1 %cosine_convert_fusion.2 = (bf16[8,1024,1024]{2,1,0:T(8,128)(2,1)}, bf16[8,1024,1024]{2,1,0:T(8,128)(2,1)}) fusion(s32[1024,1024]{1,0:T(8,128)S(1)} %dynamic-slice_bitcast_fusion.2, s32[8]{0:T(128)S(1)} %multiply_add_fusion.2), kind=kLoop, calls=%fused_computation.13.clone.1 | loop fusion | flops 134217728 | bytes 37748768 | tf_op jit(solution)/shard_map/convert
  647.8 15.5 %fusion.15 = f32[8,1024,48]{1,2,0:T(8,128)S(1)} fusion(bf16[8,48,2048]{2,1,0:T(8,128)(2,1)} %get-tuple-element.118, bf16[8,1024,1024]{2,1,0:T(8,128)(2,1)} %get-tuple-element.103, bf16[8,1024,1024]{2,1,0:T(8,128)(2,1)} %get-tuple-element.104), kind=kOutput, calls=%fused_computation.8.clone.1 | convolution fusion | flops 1677721600 | bytes 36700160 | tf_op jit(solution)/shard_map/while/body/eval_jaxpr/frk,fwk->rfw/dot_general | solution.py:37
  663.3 0.5 copy.20
  663.8 1.2 constant_dynamic-update-slice_fusion.2
  665.1 1.4 multiply_reduce_fusion
  666.5 5.6 psum.7
  672.1 52.5 %reduce-scatter.2.cloned.1.call-done = f32[1024,384]{1,0:T(8,128)} async-done(((f32[4096,384]{1,0:T(8,128)}), f32[1024,384]{1,0:T(8,128)}) %reduce-scatter.2.cloned.1.call-update) | async-done | bytes 1572880 | tf_op jit(solution)/shard_map/reduce_scatter | solution.py:58
  724.6 2.1 integer_pow.9
  726.7 0.5 copy.12
  727.2 0.7 divide_bitcast_fusion
  (13 shorter events, 0.3 us)
Async XLA Ops:
  6.5 718.1 %reduce-scatter.2.cloned.1.call-start = ((), (), s32[]{:S(2)}) async-start(), calls=%async_computation.1 | async-start | bytes 7864320 | tf_op jit(solution)/shard_map/reduce_scatter | solution.py:58
  41.9 0.9 copy-start
Sparse Core Ops, SparseCore 0:
  665.2 59.3 reduce-scatter.1
where the time goes:
time: 735 us
  other arithmetic  546 us (74%)
  matrix products  61.9 us (8%)
  waiting for transfers between devices  52.5 us (7%)
  blocking collectives  39.4 us (5%)
  local copies, waits for them, and re-layouts  21.1 us (3%)
  between operations  13.4 us (2%)
    another operation x4, other arithmetic  540 us
    dot_general x4, matrix products, one_block(): jnp.einsum('frk,fwk->rfw', replicas, spectra_matrix, preferred_element_ty...  61.9 us
    reduce_scatter x1, waiting for transfers between devices, per_device(): lax.psum_scatter(beams_for(travel, spectra_matrix, freq_count), 'chan', s...  52.5 us
    all_gather x1, blocking collectives, per_device(): gathered = lax.all_gather(masked, 'grid', axis=2, tiled=True)  33.8 us
  transfers between devices with their start and end apart: 1, of which 1 were waited for; matrix products, arithmetic and copies ran while one was open for 0% of the time, Pallas kernels for 0%

commit v1 on v0

v1 whole, which is shorter than its diff:
```python
import functools
import math

import jax
import jax.numpy as jnp
import numpy as np
from jax import lax
from jax.experimental import pallas as pl
from jax.experimental.pallas import tpu as pltpu
from jax.sharding import PartitionSpec as P

NFFT = 2048
LANES = 128
lowest_bin = 37
bin_spacing = 29

MESH = pl.DeviceIdType.MESH


def trig_tables(freq_count):
    top_bin = lowest_bin + bin_spacing * (freq_count - 1)
    lane = np.arange(LANES, dtype=np.int64)
    rows = []
    for bin_index, stride in ((top_bin, 1), (bin_spacing, 1), (bin_spacing, LANES), (top_bin, LANES)):
        angle = 2.0 * np.pi * ((bin_index * lane * stride) % NFFT) / NFFT
        rows += [np.cos(angle), np.sin(angle)]
    return np.stack(rows).astype(np.float32)


def selection_matrix(freq_count, window_count, grid_count):
    own = window_count // grid_count
    rows = np.zeros((2, freq_count, 2, window_count, grid_count, freq_count, 2, own), np.float32)
    for f in range(freq_count):
        for w in range(window_count):
            i, v = w // own, w % own
            rows[0, f, 0, w, i, f, 0, v] = 1
            rows[0, f, 1, w, i, f, 1, v] = 1
            rows[1, f, 0, w, i, f, 1, v] = -1
            rows[1, f, 1, w, i, f, 0, v] = 1
    return rows.reshape(2 * freq_count * 2 * window_count, grid_count * freq_count * 2 * own)


def window_sums(freq_count, window_count):
    return np.tile(np.eye(window_count, dtype=np.float32), (1, 2 * freq_count))


class Sizes:
    def __init__(self, rows, chans, freq_count, window_count, grid_count, chan_count):
        self.rows, self.chans = rows, chans
        self.freqs, self.windows = freq_count, window_count
        self.grid, self.chan = grid_count, chan_count
        self.chips = chan_count // 2
        self.rows_out = rows // chan_count
        self.block = math.gcd(self.rows_out, 512)
        self.blocks = self.rows_out // self.block
        self.piece = min(256, chans // 2)
        self.pieces = chans // self.piece
        self.pairs = self.pieces // 2
        self.steps = chan_count * self.blocks
        self.cols = 2 * freq_count * window_count
        self.per_f = 2 * window_count
        self.half = freq_count // 2
        self.ranges = []
        for g in range(2):
            start, end = g * self.half * self.per_f, (g + 1) * self.half * self.per_f
            self.ranges.append((start // LANES * LANES, -(-end // LANES) * LANES))
        self.width = max(hi - lo for lo, hi in self.ranges)


def make_replicas(z, tables, delays_of, out_ref):
    top_bin = lowest_bin + bin_spacing * (z.freqs - 1)

    def look(row, index):
        return jnp.take_along_axis(
            jnp.broadcast_to(tables[row : row + 1, :], index.shape), index, axis=1, mode="promise_in_bounds"
        )

    for r in range(0, z.block, 16):
        for c in range(0, z.piece, LANES):
            delay = delays_of(r, c)
            low = delay & (LANES - 1)
            high = delay >> 7
            cl, sl, ch, sh = look(2, low), look(3, low), look(4, high), look(5, high)
            cb = cl * ch - sl * sh
            sb = sl * ch + cl * sh
            c1, s1 = look(0, low), look(1, low)
            if (top_bin * LANES) % NFFT:
                ct, st = look(6, high), look(7, high)
                c1, s1 = c1 * ct - s1 * st, s1 * ct + c1 * st
            c0 = c1 * cb + s1 * sb
            s0 = s1 * cb - c1 * sb
            twice = cb + cb
            for f in reversed(range(z.freqs)):
                col = 2 * f * z.piece + c
                out_ref[r : r + 16, col : col + LANES] = c1.astype(jnp.bfloat16)
                out_ref[r : r + 16, col + z.piece : col + z.piece + LANES] = s1.astype(jnp.bfloat16)
                if f:
                    c1, c0 = c0, twice * c0 - c1
                    s1, s0 = s0, twice * s0 - s1


def kernel(z, gathered, select, tables, sums, travel, out,
           weights, rep_a, rep_b, delays, acc, mate_out, mate_in, chip_out, chip_in, norms,
           delay_sem, mate_send, mate_recv, chip_send, chip_recv, norm_send, norm_recv):
    me = lax.axis_index("chan")
    chip, core = me // 2, lax.rem(me, 2)
    mate = chip * 2 + 1 - core
    half_cols = 2 * z.half * z.piece

    barrier = pltpu.get_barrier_semaphore()
    for k in range(1, z.chan):
        pl.semaphore_signal(barrier, inc=1, device_id={"chan": lax.rem(me + k, z.chan)}, device_id_type=MESH)

    def chip_at(j):
        return lax.rem(chip + 1 + j, z.chips)

    def row_start(step):
        phase, block = step // z.blocks, lax.rem(step, z.blocks)
        j, kind = phase // 2, lax.rem(phase, 2)
        quarter = chip_at(j) * 2 + jnp.where(kind == 0, 1 - core, core)
        return pl.multiple_of(quarter * z.rows_out + block * z.block, z.block)

    def delay_copy(step):
        slot = lax.rem(step, 2)
        return pltpu.make_async_copy(
            travel.at[pl.ds(row_start(step), z.block), :], delays.at[slot], delay_sem.at[slot]
        )

    delay_copy(0).start()

    weights[...] = jnp.zeros_like(weights)
    sum_sq = jnp.zeros((z.windows, LANES), jnp.float32)
    for trig in range(2):
        for f in range(z.freqs):
            g, at = f // z.half, f % z.half
            first = (trig * z.freqs + f) * z.per_f
            part = jnp.dot(
                select[first : first + z.per_f, :], gathered[...], preferred_element_type=jnp.float32
            )
            if trig == 0:
                squared = part * part
                lanes = squared[:, 0:LANES]
                for c in range(LANES, z.chans, LANES):
                    lanes += squared[:, c : c + LANES]
                sum_sq += lanes[: z.windows] + lanes[z.windows :]
            part = part.astype(jnp.bfloat16)
            row = f * z.per_f - z.ranges[g][0]
            for p in range(z.pieces):
                col = (2 * at + trig) * z.piece
                weights[g, p, row : row + z.per_f, col : col + z.piece] = part[:, p * z.piece : (p + 1) * z.piece]
    norms[0] = sum_sq

    acc[...] = jnp.zeros_like(acc)
    delay_copy(0).wait()
    pl.semaphore_wait(barrier, z.chan - 1)

    def norm_copy(k):
        return pltpu.make_async_remote_copy(
            src_ref=norms.at[0], dst_ref=norms.at[k], send_sem=norm_send.at[k], recv_sem=norm_recv.at[k],
            device_id={"chan": lax.rem(me + k, z.chan)}, device_id_type=MESH,
        )

    for k in range(1, z.chan):
        norm_copy(k).start()

    def mate_copy(j, block):
        return pltpu.make_async_remote_copy(
            src_ref=mate_out.at[j, block], dst_ref=mate_in.at[j, block],
            send_sem=mate_send.at[j, block], recv_sem=mate_recv.at[j, block],
            device_id={"chan": mate}, device_id_type=MESH,
        )

    def chip_copy(j, block):
        return pltpu.make_async_remote_copy(
            src_ref=chip_out.at[j, block], dst_ref=chip_in.at[j, block],
            send_sem=chip_send.at[j, block], recv_sem=chip_recv.at[j, block],
            device_id={"chan": chip_at(j) * 2 + core}, device_id_type=MESH,
        )

    def multiply(rep, p):
        for g in range(2):
            lo, hi = z.ranges[g]
            acc[:, lo:hi] += lax.dot_general(
                rep[:, g * half_cols : (g + 1) * half_cols], weights[g, p, 0 : hi - lo, :],
                (((1,), (1,)), ((), ())), preferred_element_type=jnp.float32,
            )

    def replicas(slot, p, rep):
        def delays_of(r, c):
            return delays[slot, r : r + 16, pl.ds(pl.multiple_of(p * z.piece + c, LANES), LANES)]

        make_replicas(z, tables, delays_of, rep)

    replicas(0, 0, rep_a)

    def pair_step(it, carry):
        step, pair = it // z.pairs, lax.rem(it, z.pairs)
        slot = lax.rem(step, 2)
        after = jnp.minimum(it + 1, z.steps * z.pairs - 1)
        step2, pair2 = after // z.pairs, lax.rem(after, z.pairs)

        @pl.when((pair == 0) & (step + 1 < z.steps))
        def _():
            delay_copy(step + 1).start()

        multiply(rep_a, 2 * pair)
        replicas(slot, 2 * pair + 1, rep_b)

        @pl.when(step2 != step)
        def _():
            delay_copy(step2).wait()

        multiply(rep_b, 2 * pair + 1)
        replicas(lax.rem(step2, 2), 2 * pair2, rep_a)

        @pl.when(pair == z.pairs - 1)
        def _():
            phase, block = step // z.blocks, lax.rem(step, z.blocks)
            j, kind = phase // 2, lax.rem(phase, 2)

            @pl.when(kind == 0)
            def _():
                mate_out[j, block] = acc[...]
                mate_copy(j, block).start()

            @pl.when((kind == 1) & (j < z.chips - 1))
            def _():
                mate_copy(j, block).wait_recv()
                chip_out[j, block] = (acc[...] + mate_in[j, block]).astype(jnp.bfloat16)
                chip_copy(j, block).start()

            @pl.when((kind == 1) & (j == z.chips - 1))
            def _():
                mate_copy(z.chips - 1, block).wait_recv()
                beams = acc[...] + mate_in[z.chips - 1, block]
                for k in range(z.chips - 1):
                    chip_copy(k, block).wait_recv()
                    beams += chip_in[k, block].astype(jnp.float32)
                power = beams * beams
                high = power.astype(jnp.bfloat16)
                low = (power - high.astype(jnp.float32)).astype(jnp.bfloat16)
                dims = (((1,), (1,)), ((), ()))
                energy = lax.dot_general(sums[...], high, dims, preferred_element_type=jnp.float32)
                energy += lax.dot_general(sums[...], low, dims, preferred_element_type=jnp.float32)
                out[:, pl.ds(pl.multiple_of(block * z.block, z.block), z.block)] = energy

            acc[...] = jnp.zeros_like(acc)

        return carry

    lax.fori_loop(0, z.steps * z.pairs, pair_step, 0)

    for k in range(1, z.chan):
        norm_copy(k).wait()
    total = norms[0]
    for k in range(1, z.chan):
        total += norms[k]
    scale = z.freqs * z.chans * z.chan
    window_norm = jnp.sum(total, axis=1, keepdims=True) / scale + 1e-06
    out[...] = out[...] / (scale * window_norm)

    for j in range(z.chips):
        for block in range(z.blocks):
            mate_copy(j, block).wait_send()
            if j < z.chips - 1:
                chip_copy(j, block).wait_send()


def per_device(spectra, travel, quality):
    _, freq_count, own, chans = spectra.shape
    grid_count, chan_count = lax.axis_size("grid"), lax.axis_size("chan")
    z = Sizes(travel.shape[0], chans, freq_count, own * grid_count, grid_count, chan_count)
    masked = spectra * quality.astype(jnp.bfloat16)
    mine = jnp.transpose(masked, (1, 0, 2, 3)).reshape(2 * freq_count * own, chans)
    gathered = lax.all_gather(mine, "grid", axis=0, tiled=True)
    select = jnp.asarray(selection_matrix(freq_count, z.windows, grid_count), jnp.bfloat16)
    tables = jnp.asarray(trig_tables(freq_count))
    sums = jnp.asarray(window_sums(freq_count, z.windows), jnp.bfloat16)
    vmem = pl.BlockSpec(memory_space=pltpu.VMEM)
    far = max(z.chips - 1, 1)
    flops = 2 * z.rows * z.chans * z.cols * 2
    return pl.pallas_call(
        functools.partial(kernel, z),
        out_shape=jax.ShapeDtypeStruct((z.windows, z.rows_out), jnp.float32),
        in_specs=[vmem, vmem, vmem, vmem, pl.BlockSpec(memory_space=pl.ANY)],
        out_specs=vmem,
        scratch_shapes=[
            pltpu.VMEM((2, z.pieces, z.width, 2 * z.half * z.piece), jnp.bfloat16),
            pltpu.VMEM((z.block, 2 * z.freqs * z.piece), jnp.bfloat16),
            pltpu.VMEM((z.block, 2 * z.freqs * z.piece), jnp.bfloat16),
            pltpu.VMEM((2, z.block, z.chans), jnp.int32),
            pltpu.VMEM((z.block, z.cols), jnp.float32),
            pltpu.VMEM((z.chips, z.blocks, z.block, z.cols), jnp.float32),
            pltpu.VMEM((z.chips, z.blocks, z.block, z.cols), jnp.float32),
            pltpu.VMEM((far, z.blocks, z.block, z.cols), jnp.bfloat16),
            pltpu.VMEM((far, z.blocks, z.block, z.cols), jnp.bfloat16),
            pltpu.VMEM((z.chan, z.windows, LANES), jnp.float32),
            pltpu.SemaphoreType.DMA((2,)),
            pltpu.SemaphoreType.DMA((z.chips, z.blocks)),
            pltpu.SemaphoreType.DMA((z.chips, z.blocks)),
            pltpu.SemaphoreType.DMA((far, z.blocks)),
            pltpu.SemaphoreType.DMA((far, z.blocks)),
            pltpu.SemaphoreType.DMA((z.chan,)),
            pltpu.SemaphoreType.DMA((z.chan,)),
        ],
        compiler_params=pltpu.CompilerParams(
            collective_id=0, has_side_effects=True, vmem_limit_bytes=56 * 1024 * 1024
        ),
        cost_estimate=pl.CostEstimate(
            flops=flops, bytes_accessed=4 * z.rows * z.chans, transcendentals=0
        ),
        name="beam_power",
    )(gathered, select, tables, sums, travel)


def solution(mesh):
    return jax.shard_map(
        per_device,
        mesh=mesh,
        in_specs=(P(None, None, "grid", "chan"), P("grid", "chan"), P("chan")),
        out_specs=P(None, ("grid", "chan")),
        check_vma=False,
    )
```

time: 735 us -> 114 us (0.16)
  other arithmetic: 546 us -> 1.59 us
  Pallas kernels: 0 us -> 74.6 us
  matrix products: 61.9 us -> 0 us
  waiting for transfers between devices: 52.5 us -> 0 us
  local copies, waits for them, and re-layouts: 21.1 us -> 1.71 us
  between operations: 13.4 us -> 0.02 us
    another operation x4 -> x0, other arithmetic: 540 us -> none
    pallas_call x0 -> x1, Pallas kernels: none -> 74.6 us  [per_device(): pl.pallas_call(functools.partial(kernel, z), out_shape=jax.ShapeDtypeStru...]
    dot_general x4 -> x0, matrix products: 61.9 us -> none  [one_block(): jnp.einsum('frk,fwk->rfw', replicas, spectra_matrix, preferred_element_ty...]
    reduce_scatter x1 -> x0, waiting for transfers between devices: 52.5 us -> none  [per_device(): lax.psum_scatter(beams_for(travel, spectra_matrix, freq_count), 'chan', s...]
    mul x4 -> x0, local copies, waits for them, and re-layouts: 10.8 us -> none  [replica_rows(): phase_index = freq_bins[:, None, None] * delay_rows[None, :, :] % NFFT]
  transfers between devices with their start and end apart: 1 -> 0, of which waited for: 1 -> 0; matrix products, arithmetic and copies ran while one was open for 0% -> 0% of each run, Pallas kernels for 0% -> 0%
where the time goes in v1:
time: 114 us
  Pallas kernels  74.6 us (65%)
  blocking collectives  36 us (32%)
  local copies, waits for them, and re-layouts  1.71 us (2%)
  other arithmetic  1.59 us (1%)
    pallas_call x1, Pallas kernels, per_device(): pl.pallas_call(functools.partial(kernel, z), out_shape=jax.ShapeDtypeStru...  74.6 us
    all_gather x1, blocking collectives, per_device(): gathered = lax.all_gather(mine, 'grid', axis=0, tiled=True)  36 us

profile of v1, /device:TPU:0, one launch (start us, length us, event | category | flops | bytes accessed | tf_op | source)
XLA Modules:
  0.0 113.9 jit_solution(533198191754955327)
XLA Ops:
  0.0 0.7 convert_element_type.3
  0.7 0.9 multiply_bitcast_fusion
  1.6 0.1 copy.8
  1.7 0.1 reshape.4
  1.8 36.0 %all_gather.3.gathered = bf16[384,1024]{1,0:T(8,128)(2,1)} all-gather(bf16[48,1024]{1,0:T(8,128)(2,1)S(1)} %reshape.4), channel_id=1, replica_groups=mesh['grid'=8,'chan'=4] {'grid'}, dimensions={0}, use_global_device_ids=true | all-gather | bytes 884736 | tf_op jit(solution)/shard_map/all_gather | solution.py:275
  37.8 74.6 %beam_power.1 = f32[24,1024]{1,0:T(8,128)} custom-call(bf16[384,1024]{1,0:T(8,128)(2,1)} %all_gather.3.gathered, bf16[768,384]{1,0:T(8,128)(2,1)} %constant.6.clone.select, f32[8,128]{1,0:T(8,128)} %constant.7.clone.tables, bf16[24,384]{1,0:T(8,128)(2,1)} %constant.8.clone.sums, s32[4096,1024]{1,0:T(8,128)} %travel.1), custom_call_target="tpu_custom_call" | custom-call | flops 6442450944 | bytes 16777216 | tf_op jit(solution)/shard_map/beam_power/pallas_call | solution.py:282
  112.4 1.5 %copy.10 = f32[24,1024]{1,0:T(8,128)} copy(f32[24,1024]{1,0:T(8,128)} %beam_power.1) | data formatting | bytes 196608

commit v2 on v1

v2 whole, which is shorter than its diff:
```python
import functools
import math

import jax
import jax.numpy as jnp
import numpy as np
from jax import lax
from jax.experimental import pallas as pl
from jax.experimental.pallas import tpu as pltpu
from jax.sharding import PartitionSpec as P

NFFT = 2048
LANES = 128
lowest_bin = 37
bin_spacing = 29

MESH = pl.DeviceIdType.MESH


def trig_tables(freq_count):
    top_bin = lowest_bin + bin_spacing * (freq_count - 1)
    lane = np.arange(LANES, dtype=np.int64)
    rows = []
    for bin_index, stride in ((top_bin, 1), (bin_spacing, 1), (bin_spacing, LANES), (top_bin, LANES)):
        angle = 2.0 * np.pi * ((bin_index * lane * stride) % NFFT) / NFFT
        rows += [np.cos(angle), np.sin(angle)]
    return np.stack(rows).astype(np.float32)


def selection_matrix(z):
    own = z.windows // z.grid
    cols = np.zeros((2, z.grid, 2, own, z.freqs, z.freqs, 2, z.windows), np.float32)
    for f in range(z.freqs):
        for w in range(z.windows):
            i, v = w // own, w % own
            cols[0, i, 0, v, f, f, 0, w] = 1
            cols[0, i, 1, v, f, f, 1, w] = 1
            cols[1, i, 1, v, f, f, 0, w] = -1
            cols[1, i, 0, v, f, f, 1, w] = 1
    cols = cols.reshape(2, -1, z.cols)
    halves = np.zeros((2, 2, cols.shape[1], z.width), np.float32)
    for g in range(2):
        lo, hi = z.ranges[g]
        start = g * z.half * z.per_f
        end = start + z.half * z.per_f
        halves[g, :, :, start - lo : end - lo] = cols[:, :, start:end]
    return halves


def window_sums(freq_count, window_count):
    return np.tile(np.eye(window_count, dtype=np.float32), (1, 2 * freq_count))


def split_dot(left, values, terms):
    total = None
    for _ in range(terms):
        term = values.astype(jnp.bfloat16)
        product = lax.dot_general(left, term, (((1,), (1,)), ((), ())), preferred_element_type=jnp.float32)
        total = product if total is None else total + product
        values = values - term.astype(jnp.float32)
    return total


class Sizes:
    def __init__(self, rows, chans, freq_count, window_count, grid_count, chan_count):
        self.rows, self.chans = rows, chans
        self.freqs, self.windows = freq_count, window_count
        self.grid, self.chan = grid_count, chan_count
        self.chips = chan_count // 2
        self.rows_out = rows // chan_count
        self.block = math.gcd(self.rows_out, 512)
        self.blocks = self.rows_out // self.block
        self.piece = min(256, chans // 2)
        self.pieces = chans // self.piece
        self.pairs = self.pieces // 2
        self.steps = chan_count * self.blocks
        self.total = self.steps * self.pieces
        self.lead = min(5, self.total - 1)
        self.slots = (self.lead + 1) // 2
        self.cols = 2 * freq_count * window_count
        self.per_f = 2 * window_count
        self.half = freq_count // 2
        self.ranges = []
        for g in range(2):
            start, end = g * self.half * self.per_f, (g + 1) * self.half * self.per_f
            self.ranges.append((start // LANES * LANES, -(-end // LANES) * LANES))
        self.width = max(hi - lo for lo, hi in self.ranges)


def make_replicas(z, tables, delays_of, out_ref, slot, rows):
    top_bin = lowest_bin + bin_spacing * (z.freqs - 1)

    def look(row, index):
        return jnp.take_along_axis(
            jnp.broadcast_to(tables[row : row + 1, :], index.shape), index, axis=1, mode="promise_in_bounds"
        )

    for r in range(rows[0], rows[1], 16):
        for c in range(0, z.piece, LANES):
            delay = delays_of(r, c)
            low = delay & (LANES - 1)
            high = delay >> 7
            cl, sl, c1, s1 = look(2, low), look(3, low), look(0, low), look(1, low)
            ch, sh = look(4, high), look(5, high)
            cb = cl * ch - sl * sh
            sb = sl * ch + cl * sh
            if (top_bin * LANES) % NFFT:
                ct, st = look(6, high), look(7, high)
                c1, s1 = c1 * ct - s1 * st, s1 * ct + c1 * st
            c0 = c1 * cb + s1 * sb
            s0 = s1 * cb - c1 * sb
            twice = cb + cb
            for f in reversed(range(z.freqs)):
                col = 2 * f * z.piece + c
                out_ref[slot, r : r + 16, col : col + LANES] = c1.astype(jnp.bfloat16)
                out_ref[slot, r : r + 16, col + z.piece : col + z.piece + LANES] = s1.astype(jnp.bfloat16)
                if f:
                    c1, c0 = c0, twice * c0 - c1
                    s1, s0 = s0, twice * s0 - s1


def kernel(z, spectra, quality, select, tables, sums, travel, out,
           gathered, weights, rep_even, rep_odd, delays, acc, mate_out, mate_in, chip_out, chip_in, norms,
           own_send, own_recv, pass_send, pass_recv,
           delay_sem, mate_send, mate_recv, chip_send, chip_recv, norm_send, norm_recv):
    me = lax.axis_index("chan")
    slab = lax.axis_index("grid")
    chip, core = me // 2, lax.rem(me, 2)
    mate = chip * 2 + 1 - core
    next_slab = slab + 1 - 2 * lax.rem(slab, 2)
    far_slabs = z.grid // 2
    half_cols = 2 * z.half * z.piece

    barrier = pltpu.get_barrier_semaphore()
    for k in range(1, z.chan):
        pl.semaphore_signal(barrier, inc=1, device_id={"chan": lax.rem(me + k, z.chan)}, device_id_type=MESH)
    for k in range(1, far_slabs):
        pl.semaphore_signal(barrier, inc=1, device_id={"grid": lax.rem(slab + 2 * k, z.grid)}, device_id_type=MESH)
    pl.semaphore_signal(barrier, inc=1, device_id={"grid": next_slab}, device_id_type=MESH)

    def chip_at(j):
        return lax.rem(chip + 1 + j, z.chips)

    def row_start(step):
        phase, block = step // z.blocks, lax.rem(step, z.blocks)
        j, kind = phase // 2, lax.rem(phase, 2)
        quarter = chip_at(j) * 2 + jnp.where(kind == 0, 1 - core, core)
        return pl.multiple_of(quarter * z.rows_out + block * z.block, z.block)

    def delay_copy(step):
        slot = lax.rem(step, 2)
        return pltpu.make_async_copy(
            travel.at[pl.ds(row_start(step), z.block), :], delays.at[slot], delay_sem.at[slot]
        )

    delay_copy(0).start()
    delay_copy(1).start()

    gathered[slab] = spectra[...] * quality[...].astype(jnp.bfloat16)
    pl.semaphore_wait(barrier, z.chan - 1 + far_slabs)

    def own_copy(k):
        target = next_slab if k == 0 else lax.rem(slab + 2 * k, z.grid)
        return pltpu.make_async_remote_copy(
            src_ref=gathered.at[slab], dst_ref=gathered.at[slab],
            send_sem=own_send.at[k], recv_sem=own_recv.at[k],
            device_id={"grid": target}, device_id_type=MESH,
        )

    def own_arrival(k):
        source = next_slab if isinstance(k, int) and k == 0 else lax.rem(slab + z.grid - 2 * k, z.grid)
        return pltpu.make_async_remote_copy(
            src_ref=gathered.at[source], dst_ref=gathered.at[source],
            send_sem=own_send.at[k], recv_sem=own_recv.at[k],
            device_id={"grid": next_slab}, device_id_type=MESH,
        )

    def pass_copy(k):
        source = lax.rem(slab + z.grid - 2 * k, z.grid)
        return pltpu.make_async_remote_copy(
            src_ref=gathered.at[source], dst_ref=gathered.at[source],
            send_sem=pass_send.at[k], recv_sem=pass_recv.at[k],
            device_id={"grid": next_slab}, device_id_type=MESH,
        )

    def pass_arrival(k):
        source = lax.rem(next_slab + z.grid - 2 * k, z.grid)
        return pltpu.make_async_remote_copy(
            src_ref=gathered.at[source], dst_ref=gathered.at[source],
            send_sem=pass_send.at[k], recv_sem=pass_recv.at[k],
            device_id={"grid": next_slab}, device_id_type=MESH,
        )

    near_first = sorted(range(1, far_slabs), key=lambda k: min(k, far_slabs - k))
    for k in near_first:
        own_copy(k).start()
    own_copy(0).start()

    def replicas(piece, rep, rows):
        slot, p = lax.rem(piece // z.pieces, 2), lax.rem(piece, z.pieces)

        def delays_of(r, c):
            return delays[slot, r : r + 16, pl.ds(pl.multiple_of(p * z.piece + c, LANES), LANES)]

        make_replicas(z, tables, delays_of, rep, lax.rem(piece // 2, z.slots), rows)

    def delays_ready(piece):
        @pl.when(lax.rem(piece, z.pieces) == 0)
        def _():
            delay_copy(piece // z.pieces).wait()

    def delays_used(piece):
        after = piece // z.pieces + 2

        @pl.when((lax.rem(piece, z.pieces) == z.pieces - 1) & (after < z.steps))
        def _():
            delay_copy(after).start()

    def early(piece, carry):
        @pl.when(lax.rem(piece, 2) == 0)
        def _():
            delays_ready(piece)
            replicas(piece, rep_even, (0, z.block))

        @pl.when(lax.rem(piece, 2) == 1)
        def _():
            replicas(piece, rep_odd, (0, z.block))
            delays_used(piece)

        return carry

    spots = [z.lead * (n + 1) // (len(near_first) + 2) for n in range(len(near_first))]
    done = 0
    for k, spot in zip(near_first, spots):
        if spot > done:
            lax.fori_loop(done, spot, early, 0)
            done = spot
        own_arrival(k).wait_recv()
        pass_copy(k).start()
    lax.fori_loop(done, z.lead, early, 0)

    own_arrival(0).wait_recv()
    for k in near_first:
        pass_arrival(k).wait_recv()

    spectra_rows = gathered[...].reshape(z.grid * gathered.shape[1], z.chans)
    for g in range(2):
        lo, hi = z.ranges[g]
        lane = lax.broadcasted_iota(jnp.int32, (z.piece, hi - lo), 1) + lo
        sum_sq = jnp.zeros((8, hi - lo), jnp.float32)
        for trig in range(2):
            for p in range(z.pieces):
                part = lax.dot_general(
                    spectra_rows[:, p * z.piece : (p + 1) * z.piece], select[g, trig, :, 0 : hi - lo],
                    (((0,), (0,)), ((), ())), preferred_element_type=jnp.float32,
                )
                if trig == 0:
                    sum_sq += jnp.sum((part * part).reshape(z.piece // 8, 8, hi - lo), axis=0)
                for at in range(z.half):
                    first = (g * z.half + at) * z.per_f
                    row = (2 * at + trig) * z.piece
                    chosen = jnp.where((lane >= first) & (lane < first + z.per_f), part, 0.0)
                    weights[g, p, row : row + z.piece, 0 : hi - lo] = chosen.astype(jnp.bfloat16)
        if g == 0:
            norms[0, :, lo:hi] = sum_sq
            norms[0, :, hi:] = jnp.zeros((8, z.cols - hi), jnp.float32)
        else:
            norms[0, :, lo:hi] += sum_sq

    acc[...] = jnp.zeros_like(acc)

    def norm_copy(k):
        return pltpu.make_async_remote_copy(
            src_ref=norms.at[0], dst_ref=norms.at[k], send_sem=norm_send.at[k], recv_sem=norm_recv.at[k],
            device_id={"chan": lax.rem(me + k, z.chan)}, device_id_type=MESH,
        )

    for k in range(1, z.chan):
        norm_copy(k).start()

    def mate_copy(j, block):
        return pltpu.make_async_remote_copy(
            src_ref=mate_out.at[j, block], dst_ref=mate_in.at[j, block],
            send_sem=mate_send.at[j, block], recv_sem=mate_recv.at[j, block],
            device_id={"chan": mate}, device_id_type=MESH,
        )

    def chip_copy(j, block):
        return pltpu.make_async_remote_copy(
            src_ref=chip_out.at[j, block], dst_ref=chip_in.at[j, block],
            send_sem=chip_send.at[j, block], recv_sem=chip_recv.at[j, block],
            device_id={"chan": chip_at(j) * 2 + core}, device_id_type=MESH,
        )

    def multiply(rep, piece, during):
        slot, p = lax.rem(piece // 2, z.slots), lax.rem(piece, z.pieces)
        for g in range(2):
            lo, hi = z.ranges[g]
            acc[:, lo:hi] += lax.dot_general(
                rep[slot, :, g * half_cols : (g + 1) * half_cols], weights[g, p, :, 0 : hi - lo],
                (((1,), (0,)), ((), ())), preferred_element_type=jnp.float32,
            )
            during(g)

    def turn(piece, rep, ahead_rep):
        ahead = piece + z.lead

        @pl.when(ahead < z.total)
        def _():
            def during(g):
                replicas(ahead, ahead_rep, (g * z.block // 2, (g + 1) * z.block // 2))

            multiply(rep, piece, during)

        @pl.when(ahead >= z.total)
        def _():
            multiply(rep, piece, lambda g: None)

    def pair_step(it, carry):
        step, pair = it // z.pairs, lax.rem(it, z.pairs)

        turn(2 * it, rep_even, rep_odd)
        delays_used(2 * it + z.lead)

        @pl.when(2 * it + 1 + z.lead < z.total)
        def _():
            delays_ready(2 * it + 1 + z.lead)

        turn(2 * it + 1, rep_odd, rep_even)

        @pl.when(pair == z.pairs - 1)
        def _():
            phase, block = step // z.blocks, lax.rem(step, z.blocks)
            j, kind = phase // 2, lax.rem(phase, 2)

            @pl.when(kind == 0)
            def _():
                mate_out[j, block] = acc[...]
                mate_copy(j, block).start()

            @pl.when((kind == 1) & (j < z.chips - 1))
            def _():
                mate_copy(j, block).wait_recv()
                chip_out[j, block] = (acc[...] + mate_in[j, block]).astype(jnp.bfloat16)
                chip_copy(j, block).start()

            @pl.when((kind == 1) & (j == z.chips - 1))
            def _():
                mate_copy(z.chips - 1, block).wait_recv()
                beams = acc[...] + mate_in[z.chips - 1, block]
                for k in range(z.chips - 1):
                    chip_copy(k, block).wait_recv()
                    beams += chip_in[k, block].astype(jnp.float32)
                energy = split_dot(sums[...], beams * beams, 2)
                out[:, pl.ds(pl.multiple_of(block * z.block, z.block), z.block)] = energy

            acc[...] = jnp.zeros_like(acc)

        return carry

    lax.fori_loop(0, z.steps * z.pairs, pair_step, 0)

    for k in range(1, z.chan):
        norm_copy(k).wait()
    total = norms[0]
    for k in range(1, z.chan):
        total += norms[k]
    scale = z.freqs * z.chans * z.chan
    window_norm = jnp.sum(split_dot(sums[...], total, 3), axis=1, keepdims=True) / scale + 1e-06
    out[...] = out[...] / (scale * window_norm)

    own_copy(0).wait_send()
    for k in near_first:
        own_copy(k).wait_send()
        pass_copy(k).wait_send()
    for j in range(z.chips):
        for block in range(z.blocks):
            mate_copy(j, block).wait_send()
            if j < z.chips - 1:
                chip_copy(j, block).wait_send()


def per_device(spectra, travel, quality):
    _, freq_count, own, chans = spectra.shape
    grid_count, chan_count = lax.axis_size("grid"), lax.axis_size("chan")
    z = Sizes(travel.shape[0], chans, freq_count, own * grid_count, grid_count, chan_count)
    mine = jnp.transpose(spectra, (0, 2, 1, 3)).reshape(2 * own * freq_count, chans)
    select = jnp.asarray(selection_matrix(z), jnp.bfloat16)
    tables = jnp.asarray(trig_tables(freq_count))
    sums = jnp.asarray(window_sums(freq_count, z.windows), jnp.bfloat16)
    vmem = pl.BlockSpec(memory_space=pltpu.VMEM)
    far = max(z.chips - 1, 1)
    flops = 2 * z.rows * z.chans * z.cols * 2
    return pl.pallas_call(
        functools.partial(kernel, z),
        out_shape=jax.ShapeDtypeStruct((z.windows, z.rows_out), jnp.float32),
        in_specs=[vmem, vmem, vmem, vmem, vmem, pl.BlockSpec(memory_space=pl.ANY)],
        out_specs=vmem,
        scratch_shapes=[
            pltpu.VMEM((grid_count, 2 * own * freq_count, chans), jnp.bfloat16),
            pltpu.VMEM((2, z.pieces, 2 * z.half * z.piece, z.width), jnp.bfloat16),
            pltpu.VMEM((z.slots, z.block, 2 * z.freqs * z.piece), jnp.bfloat16),
            pltpu.VMEM((z.slots, z.block, 2 * z.freqs * z.piece), jnp.bfloat16),
            pltpu.VMEM((2, z.block, z.chans), jnp.int32),
            pltpu.VMEM((z.block, z.cols), jnp.float32),
            pltpu.VMEM((z.chips, z.blocks, z.block, z.cols), jnp.float32),
            pltpu.VMEM((z.chips, z.blocks, z.block, z.cols), jnp.float32),
            pltpu.VMEM((far, z.blocks, z.block, z.cols), jnp.bfloat16),
            pltpu.VMEM((far, z.blocks, z.block, z.cols), jnp.bfloat16),
            pltpu.VMEM((z.chan, 8, z.cols), jnp.float32),
            pltpu.SemaphoreType.DMA((grid_count // 2,)),
            pltpu.SemaphoreType.DMA((grid_count // 2,)),
            pltpu.SemaphoreType.DMA((grid_count // 2,)),
            pltpu.SemaphoreType.DMA((grid_count // 2,)),
            pltpu.SemaphoreType.DMA((2,)),
            pltpu.SemaphoreType.DMA((z.chips, z.blocks)),
            pltpu.SemaphoreType.DMA((z.chips, z.blocks)),
            pltpu.SemaphoreType.DMA((far, z.blocks)),
            pltpu.SemaphoreType.DMA((far, z.blocks)),
            pltpu.SemaphoreType.DMA((z.chan,)),
            pltpu.SemaphoreType.DMA((z.chan,)),
        ],
        compiler_params=pltpu.CompilerParams(
            collective_id=0, has_side_effects=True, vmem_limit_bytes=56 * 1024 * 1024
        ),
        cost_estimate=pl.CostEstimate(
            flops=flops, bytes_accessed=4 * z.rows * z.chans, transcendentals=0
        ),
        name="beam_power",
    )(mine, quality.reshape(1, chans), select, tables, sums, travel)


def solution(mesh):
    return jax.shard_map(
        per_device,
        mesh=mesh,
        in_specs=(P(None, None, "grid", "chan"), P("grid", "chan"), P("chan")),
        out_specs=P(None, ("grid", "chan")),
        check_vma=False,
    )
```

time: 114 us -> 85.1 us (0.75)
  blocking collectives: 36 us -> 0 us
  Pallas kernels: 74.6 us -> 83.4 us
  other arithmetic: 1.59 us -> 0 us
    all_gather x1 -> x0, blocking collectives: 36 us -> none  [per_device(): gathered = lax.all_gather(mine, 'grid', axis=0, tiled=True)]
    pallas_call x1, Pallas kernels: 74.6 us -> 83.4 us  [per_device(): pl.pallas_call(functools.partial(kernel, z), out_shape=jax.ShapeDtypeStru...]
where the time goes in v2:
time: 85.1 us; the launch traced here: 85 us
  Pallas kernels  83.4 us (98%)
  local copies, waits for them, and re-layouts  1.54 us (2%)
    pallas_call x1, Pallas kernels, per_device(): pl.pallas_call(functools.partial(kernel, z), out_shape=jax.ShapeDtypeStru...  83.4 us

profile of v2, /device:TPU:0, one launch (start us, length us, event | category | flops | bytes accessed | tf_op | source)
XLA Modules:
  0.0 85.0 jit_solution(16956848593317865556)
XLA Ops:
  0.0 83.4 %beam_power.1 = f32[24,1024]{1,0:T(8,128)} custom-call(bf16[48,1024]{1,0:T(8,128)(2,1)} %bitcast.4, s32[1,1024]{1,0:T(1,128)} %bitcast.5, bf16[2,2,384,256]{3,2,1,0:T(8,128)(2,1)} %constant.6.clone.select, f32[8,128]{1,0:T(8,128)} %constant.7.clone.tables, bf16[24,384]{1,0:T(8,128)(2,1)} %constant.8.clone.sums, s32[4096,1024]{1,0:T(8,128)} %travel.1), custom_call_target="tpu_custom_call" | custom-call | flops 6442450944 | bytes 16777216 | tf_op jit(solution)/shard_map/beam_power/pallas_call | solution.py:394
  83.4 1.5 %copy.8 = f32[24,1024]{1,0:T(8,128)} copy(f32[24,1024]{1,0:T(8,128)} %beam_power.1) | data formatting | bytes 196608

commit v3 on v2

--- a/solution.py
+++ b/solution.py
@@ -17,12 +17,23 @@
 MESH = pl.DeviceIdType.MESH
 
 
+SINE = (6.28318527371, -10.335419365544, 5.100139396896, -1.1964839648, 0.155120274432)
+COSINE = (0.999999953467, -4.934792858676, 4.05841189832, -1.331880161216, 0.219696798464)
+
+
+def polynomial(square, coefficients):
+    value = coefficients[-1]
+    for coefficient in coefficients[-2::-1]:
+        value = value * square + coefficient
+    return value
+
+
 def trig_tables(freq_count):
     top_bin = lowest_bin + bin_spacing * (freq_count - 1)
     lane = np.arange(LANES, dtype=np.int64)
     rows = []
-    for bin_index, stride in ((top_bin, 1), (bin_spacing, 1), (bin_spacing, LANES), (top_bin, LANES)):
-        angle = 2.0 * np.pi * ((bin_index * lane * stride) % NFFT) / NFFT
+    for stride in (1, LANES):
+        angle = 2.0 * np.pi * ((top_bin * lane * stride) % NFFT) / NFFT
         rows += [np.cos(angle), np.sin(angle)]
     return np.stack(rows).astype(np.float32)
 
@@ -99,17 +110,20 @@
         for c in range(0, z.piece, LANES):
             delay = delays_of(r, c)
             low = delay & (LANES - 1)
-            high = delay >> 7
-            cl, sl, c1, s1 = look(2, low), look(3, low), look(0, low), look(1, low)
-            ch, sh = look(4, high), look(5, high)
-            cb = cl * ch - sl * sh
-            sb = sl * ch + cl * sh
+            c1, s1 = look(0, low), look(1, low)
             if (top_bin * LANES) % NFFT:
-                ct, st = look(6, high), look(7, high)
+                high = delay >> 7
+                ct, st = look(2, high), look(3, high)
                 c1, s1 = c1 * ct - s1 * st, s1 * ct + c1 * st
+            turns = delay.astype(jnp.float32) * (bin_spacing / NFFT)
+            u = turns - lax.round(turns, lax.RoundingMethod.TO_NEAREST_EVEN)
+            square = u * u
+            twice_sin = u * polynomial(square, SINE)
+            twice = 2.0 - twice_sin * twice_sin
+            cb = 0.5 * twice
+            sb = twice_sin * polynomial(square, COSINE)
             c0 = c1 * cb + s1 * sb
             s0 = s1 * cb - c1 * sb
-            twice = cb + cb
             for f in reversed(range(z.freqs)):
                 col = 2 * f * z.piece + c
                 out_ref[slot, r : r + 16, col : col + LANES] = c1.astype(jnp.bfloat16)

time: 85.1 us -> 93.3 us (1.096)
  Pallas kernels: 83.4 us -> 91.6 us
    pallas_call x1, Pallas kernels: 83.4 us -> 91.6 us  [per_device(): pl.pallas_call(functools.partial(kernel, z), out_shape=jax.ShapeDtypeStru...]
where the time goes in v3:
time: 93.3 us; the launch traced here: 93.1 us
  Pallas kernels  91.6 us (98%)
  local copies, waits for them, and re-layouts  1.54 us (2%)
    pallas_call x1, Pallas kernels, per_device(): pl.pallas_call(functools.partial(kernel, z), out_shape=jax.ShapeDtypeStru...  91.6 us

profile of v3, /device:TPU:0, one launch (start us, length us, event | category | flops | bytes accessed | tf_op | source)
XLA Modules:
  0.0 93.1 jit_solution(1963341973897079632)
XLA Ops:
  0.0 91.6 %beam_power.1 = f32[24,1024]{1,0:T(8,128)} custom-call(bf16[48,1024]{1,0:T(8,128)(2,1)} %bitcast.4, s32[1,1024]{1,0:T(1,128)} %bitcast.5, bf16[2,2,384,256]{3,2,1,0:T(8,128)(2,1)} %constant.6.clone.select, f32[4,128]{1,0:T(4,128)} %constant.7.clone.tables, bf16[24,384]{1,0:T(8,128)(2,1)} %constant.8.clone.sums, s32[4096,1024]{1,0:T(8,128)} %travel.1), custom_call_target="tpu_custom_call" | custom-call | flops 6442450944 | bytes 16777216 | tf_op jit(solution)/shard_map/beam_power/pallas_call | solution.py:408
  91.6 1.5 %copy.8 = f32[24,1024]{1,0:T(8,128)} copy(f32[24,1024]{1,0:T(8,128)} %beam_power.1) | data formatting | bytes 196608
